TPU v7x, 512 devices: a whole 4x4x16 slice. The times are simulated.
512 devices in a mesh: dp: 32 (over x, z_hi, core), tensor: 16 (over y, z_lo).
Axes of the slice: x: 4, y: 4, z: 16 (z_hi: 4, z_lo: 4; z = z_hi * 4 + z_lo), core: 2. Of those that a mesh axis runs over, the one named last changes fastest.
Arguments:
- tokens: bfloat16 [4096, 4096], P('dp', 'tensor'), may hold values from -6 to 6
- weight: bfloat16 [4096, 14336], P('dp', 'tensor'), may hold values from -0.09375 to 0.09375
- cotangent: bfloat16 [4096, 14336], P('dp', 'tensor'), may hold values from -6 to 6
- levels: int32 [28], replicated, may hold values from 0 to 8
Outputs:
- output: bfloat16 [4096, 14336], P('dp', 'tensor')
- input_grad: bfloat16 [4096, 4096], P('dp', 'tensor')
- weight_grad: float32 [4096, 14336], P('dp', 'tensor')
All inputs are finite; a program needn't handle non-finite values.
Results may differ from a plain program's by a relative error of at most 0.022.
Values may be sent and summed in bfloat16 or wider, within the bound.
No kernel may reach another device: no remote copies, remote signals or barrier semaphores. Data moves between devices by JAX's collectives and lax.ppermute only.
A program may use at most 128 MiB of HBM per device.

v0:
```python
import jax
import jax.numpy as jnp
from jax import lax
from jax.experimental.layout import Layout, with_layout_constraint
from jax.sharding import PartitionSpec as P

BLOCK = 512
RING = 4
GROUPS = 16


def dp_of(x, z, core):
    return ((x % RING) * RING + z % RING) * 2 + core


def swap_pairs():
    return [
        (
            dp_of(y, z, core) * GROUPS + x * RING + low,
            dp_of(x, z, core) * GROUPS + y * RING + low,
        )
        for x in range(RING)
        for z in range(RING)
        for core in range(2)
        for y in range(RING)
        for low in range(RING)
    ]


def dp_pairs(dx, flip):
    return [
        (dp_of(x + dx, z, core ^ flip), dp_of(x, z, core))
        for x in range(RING)
        for z in range(RING)
        for core in range(2)
    ]


def groups_x():
    return [[dp_of(x, z, core) for x in range(RING)] for z in range(RING) for core in range(2)]


def groups_z():
    return [[dp_of(x, z, core) for z in range(RING)] for x in range(RING) for core in range(2)]


def groups_y():
    return [[y * RING + low for y in range(RING)] for low in range(RING)]


def groups_core_low():
    return [
        [
            dp_of(x, z, core) * GROUPS + y * RING + low
            for low in range(RING)
            for core in range(2)
        ]
        for x in range(RING)
        for z in range(RING)
        for y in range(RING)
    ]


def from_core(block):
    return lax.ppermute(block, "dp", dp_pairs(0, 1))


def from_x(block, shift):
    return lax.ppermute(block, "dp", dp_pairs(shift, 0))


def swap(block):
    return lax.ppermute(block, ("dp", "tensor"), swap_pairs())


def row_major(array):
    return with_layout_constraint(array, Layout(major_to_minor=tuple(range(array.ndim))))


def exchange(parts, axis, groups):
    parts = row_major(parts)
    return row_major(lax.all_to_all(parts, axis, 0, 0, axis_index_groups=groups, tiled=True))


def collect(block, axis, groups):
    return exchange(jnp.broadcast_to(block[None], (len(groups[0]),) + block.shape), axis, groups)


def total(parts):
    return jnp.sum(parts.astype(jnp.float32), axis=0)


def block_of(steps, index, *operands):
    shapes = jax.eval_shape(steps, *operands)

    def nothing(*_):
        return jax.tree.map(lambda leaf: jnp.zeros(leaf.shape, leaf.dtype), shapes)

    return lax.cond(index >= 0, steps, nothing, *operands)


def near_first(pair, core):
    return jnp.where(core == 0, pair, pair[::-1])


def on_device(tokens, weight, cotangent, levels):
    token_rows, local_features = tokens.shape
    local_cols = weight.shape[1]
    half = local_features // 2
    dp_count = lax.axis_size("dp")
    dp = lax.axis_index("dp")
    core = dp % 2
    x = dp // (2 * RING)
    tensor = lax.axis_index("tensor")
    wide = jnp.float32
    narrow = jnp.bfloat16

    col_start = tensor * local_cols
    column_ids = col_start + jnp.arange(local_cols, dtype=jnp.int32)
    block_ids = column_ids // BLOCK
    block_range = jnp.arange(levels.shape[0], dtype=jnp.int32)
    membership = (block_ids[None, :] == block_range[:, None]).astype(wide)
    level_vals = levels.astype(wide) / 8.0
    col_scale = jnp.sum(membership * level_vals[:, None], axis=0)

    scaled = (cotangent.astype(wide) * col_scale[None, :]).astype(narrow)
    scaled_pair = jnp.concatenate([scaled, from_core(scaled)], axis=0)
    scaled_pair, tokens = lax.optimization_barrier((scaled_pair, tokens))
    scaled_all = lax.all_gather(scaled_pair, "dp", axis=0, axis_index_groups=groups_x(), tiled=True)

    both = ("dp", "tensor")

    crossed = swap(tokens)
    parts = jnp.stack([crossed[:, :half], crossed[:, half:]])
    parts = jnp.broadcast_to(parts[None], (RING, 2, token_rows, half))
    line = exchange(parts.reshape(2 * RING, token_rows, half), both, groups_core_low())
    line = line.reshape(RING, 2, token_rows, half)
    line = jnp.concatenate([line[i] for i in range(RING)], axis=2)
    line = near_first(line, core)
    line, weight = lax.optimization_barrier((line, weight))
    brick = collect(line, "tensor", groups_y()).reshape(-1, RING * half)

    weight_line = lax.all_gather(weight, "dp", axis=0, axis_index_groups=groups_z(), tiled=True)
    brick, weight_line = lax.optimization_barrier((brick, weight_line))

    grads = lax.dot_general(brick, scaled_all, (((0,), (0,)), ((), ())), preferred_element_type=wide)
    grads = grads.astype(narrow)
    grads, brick, weight_line = lax.optimization_barrier((grads, brick, weight_line))
    grads = lax.psum_scatter(
        grads, "dp", scatter_dimension=0, axis_index_groups=groups_z(), tiled=True
    )
    grad_factor = 1.0 / jnp.sqrt(jnp.float32(token_rows * dp_count))
    weight_grad = grads.astype(wide) * grad_factor

    def sums(scaled_all, brick, weight_line):
        term = lax.dot_general(scaled_all, weight_line, (((1,), (1,)), ((), ())), preferred_element_type=wide)
        term = row_major(term.astype(narrow)).reshape(RING, 2, token_rows, RING * half)
        term = near_first(total(exchange(term, "tensor", groups_y())).astype(narrow), core)
        term = jnp.stack([term[:, :, i * half:(i + 1) * half] for i in range(RING)])

        share = jnp.dot(brick, weight_line, preferred_element_type=wide)
        share = share.reshape(RING, 2, token_rows, local_cols)
        other = from_core(share[:, 1].astype(narrow))
        pieces = []
        for i in range(RING):
            at = (x + i) % RING
            piece = lax.dynamic_index_in_dim(share[:, 0], at, 0, keepdims=False)
            pieces.append(piece + lax.dynamic_index_in_dim(other, at, 0, keepdims=False).astype(wide))
        near = pieces[0]
        away = [piece.astype(narrow) for piece in pieces[1:]]
        away, term = lax.optimization_barrier((away, term))
        running = near
        for i in range(1, RING):
            running += from_x(away[i - 1], -i).astype(wide)

        term = exchange(term.reshape(2 * RING, token_rows, half), both, groups_core_low())
        term = total(term.reshape(RING, 2, token_rows, half)).astype(narrow)
        input_grad = swap(jnp.concatenate([term[0], term[1]], axis=1))
        return running, input_grad

    running, input_grad = block_of(sums, dp, scaled_all, brick, weight_line)
    output = (running * col_scale[None, :]).astype(narrow)
    return (output, input_grad, weight_grad)


def solution(mesh):
    placed = (P("dp", "tensor"), P("dp", "tensor"), P("dp", "tensor"), P())
    return jax.shard_map(
        on_device,
        mesh=mesh,
        in_specs=placed,
        out_specs=(P("dp", "tensor"), P("dp", "tensor"), P("dp", "tensor")),
        check_vma=False,
    )
```

profile of v0, /device:TPU:6, one launch (start us, length us, event | category | flops | bytes accessed | tf_op | source)
XLA Modules:
  0.0 166.1 jit_solution(17490993675358682100)
XLA Ops:
  7.2 0.0 copy-start.1
  7.2 0.0 all-gather.2.cloned.1.call-start
  7.2 0.7 convert_multiply_fusion.1
  7.9 0.1 select_reduce_fusion
  8.0 1.0 multiply_convert_fusion.1
  9.0 1.9 %collective-permute-start.5 = (bf16[128,896]{1,0:T(8,128)(2,1)S(1)}, bf16[128,896]{1,0:T(8,128)(2,1)S(1)}, u32[]{:S(2)}, u32[]{:S(2)}) collective-permute-start(bf16[128,896]{1,0:T(8,128)(2,1)S(1)} %multiply_convert_fusion.1), channel_id=1, source_target_pairs={{16,0},{0,16},{48,32},{32,48},{80,64},{64,80},{112,96},{96,112},{1... | collective-permute-start | bytes 688136 | tf_op jit(solution)/shard_map/ppermute | solution.py:65
  10.9 1.5 collective-permute-done.5
  12.4 0.8 pad_maximum_fusion.2
  13.2 0.0 all-gather.2.cloned.1.call-update
  13.2 0.0 copy-done.1
  13.2 4.8 %collective-permute-start.6 = (bf16[128,256]{1,0:T(8,128)(2,1)S(1)}, bf16[128,256]{1,0:T(8,128)(2,1)S(1)}, u32[]{:S(2)}, u32[]{:S(2)}) collective-permute-start(bf16[128,256]{1,0:T(8,128)(2,1)S(1)} %copy-done.1), channel_id=1, source_target_pairs={{0,0},{1,1},{2,2},{3,3},{128,4},{129,5},{130,6},{131,7},{256,8},{2... | collective-permute-start | bytes 196616 | tf_op jit(solution)/shard_map/ppermute | solution.py:73
  18.0 6.0 %collective-permute-done.6 = bf16[128,256]{1,0:T(8,128)(2,1)S(1)} collective-permute-done((bf16[128,256]{1,0:T(8,128)(2,1)S(1)}, bf16[128,256]{1,0:T(8,128)(2,1)S(1)}, u32[]{:S(2)}, u32[]{:S(2)}) %collective-permute-start.6) | collective-permute-done | bytes 65568 | tf_op jit(solution)/shard_map/ppermute | solution.py:73
  24.1 0.8 broadcast_in_dim.4
  24.9 5.9 %all-to-all-start.2 = ((bf16[8,128,128]{2,1,0:T(8,128)(2,1)}), bf16[8,128,128]{2,1,0:T(8,128)(2,1)S(1)}, u32[]{:S(2)}, u32[]{:S(2)}) async-start(bf16[8,128,128]{2,1,0:T(8,128)(2,1)} %bitcast.21), calls=%async_computation.2 | async-start | bytes 524288 | tf_op jit(solution)/shard_map/all_to_all | solution.py:82
  30.8 9.7 %all-to-all-done.2 = bf16[8,128,128]{2,1,0:T(8,128)(2,1)S(1)} async-done(((bf16[8,128,128]{2,1,0:T(8,128)(2,1)}), bf16[8,128,128]{2,1,0:T(8,128)(2,1)S(1)}, u32[]{:S(2)}, u32[]{:S(2)}) %all-to-all-start.2) | async-done | bytes 262176 | tf_op jit(solution)/shard_map/all_to_all | solution.py:82
  40.6 0.0 copy-start
  40.6 1.1 broadcast_in_dim.5
  41.7 3.5 %all-to-all-start.3 = ((bf16[4,2,128,512]{3,2,1,0:T(8,128)(2,1)}), bf16[4,2,128,512]{3,2,1,0:T(8,128)(2,1)S(1)}, u32[]{:S(2)}, u32[]{:S(2)}) async-start(bf16[4,2,128,512]{3,2,1,0:T(8,128)(2,1)} %broadcast_in_dim.5), calls=%async_computation.3 | async-start | bytes 2097152 | tf_op jit(solution)/shard_map/all_to_all | solution.py:82
  45.2 0.0 reduce-scatter.2.cloned.1.call-start
  45.3 0.0 copy-done
  45.3 42.4 %all_gather.6 = bf16[512,896]{1,0:T(8,128)(2,1)S(1)} all-gather(bf16[128,896]{1,0:T(8,128)(2,1)S(1)} %copy-done), channel_id=1, replica_groups={{0,32,64,96},{16,48,80,112},{128,160,192,224},{144,176,208,240},{256,28..., dimensions={0}, use_global_device_ids=true | all-gather | bytes 1146880 | tf_op jit(solution)/shard_map/all_gather | solution.py:143
  87.7 0.0 all-to-all-done.3
  87.7 0.0 all-gather.2.cloned.1.call-done
  87.7 3.7 %convolution_convert_fusion.1 = bf16[512,896]{1,0:T(8,128)(2,1)} fusion(bf16[1024,512]{1,0:T(8,128)(2,1)S(1)} %bitcast.52, bf16[1024,896]{1,0:T(8,128)(2,1)} %all-gather.2.cloned.1.call-done), kind=kOutput, calls=%fused_computation.22 | convolution fusion | flops 939982848 | bytes 3801088 | tf_op jit(solution)/shard_map/dot_general | solution.py:146
  91.4 0.0 reduce-scatter.2.cloned.1.call-update
  91.5 63.9 %conditional.1 = (f32[128,896]{1,0:T(8,128)S(1)}, bf16[128,256]{1,0:T(8,128)(2,1)}) conditional(s32[]{:T(128)} %convert_element_type.75, () %tuple.23, (bf16[1024,512]{1,0:T(8,128)(2,1)S(1)}, bf16[512,896]{1,0:T(8,128)(2,1)S(1)}, s32[]{:T(128)}, s32[]{:T(128)}, pred[]{:T(512)}, /*index=5*/s32[]{:T(128)}, bf16[1024,896]{1,0:T(8,128)(2,1)}) %tuple.48), branch_computations={%region_1.2_spmd, %region_2.5_spmd} | conditional | flops 1882669056 | bytes 33621000 | solution.py:99
  91.5 3.8 %convolution_convert_fusion = bf16[1024,512]{1,0:T(8,128)(2,1)} fusion(bf16[1024,896]{1,0:T(8,128)(2,1)} %get-tuple-element.42, bf16[512,896]{1,0:T(8,128)(2,1)S(1)} %get-tuple-element.37), kind=kOutput, calls=%fused_computation.1 | convolution fusion | flops 940048384 | bytes 3801088 | tf_op jit(solution)/shard_map/cond/branch_1_fun/dot_general | solution.py:156
  95.2 4.6 %all-to-all-start = ((bf16[4,2,128,512]{3,2,1,0:T(8,128)(2,1)}), bf16[4,2,128,512]{3,2,1,0:T(8,128)(2,1)}, u32[]{:S(2)}, u32[]{:S(2)}) async-start(bf16[4,2,128,512]{3,2,1,0:T(8,128)(2,1)} %bitcast.10), calls=%async_computation | async-start | bytes 2097152 | tf_op jit(solution)/shard_map/cond/branch_1_fun/all_to_all | solution.py:82
  99.9 1.2 fusion.11
  101.1 0.1 fusion
  101.2 1.9 %collective-permute-start = (bf16[4,128,896]{2,1,0:T(8,128)(2,1)S(1)}, bf16[4,128,896]{2,1,0:T(8,128)(2,1)}, u32[]{:S(2)}, u32[]{:S(2)}) collective-permute-start(bf16[4,128,896]{2,1,0:T(8,128)(2,1)S(1)} %fusion), channel_id=1, source_target_pairs={{16,0},{0,16},{48,32},{32,48},{80,64},{64,80},{112,96},{96,112},{1... | collective-permute-start | bytes 2752520 | tf_op jit(solution)/shard_map/cond/branch_1_fun/ppermute | solution.py:65
  103.1 0.1 slice.56
  103.4 11.7 %all-to-all-done = bf16[4,2,128,512]{3,2,1,0:T(8,128)(2,1)} async-done(((bf16[4,2,128,512]{3,2,1,0:T(8,128)(2,1)}), bf16[4,2,128,512]{3,2,1,0:T(8,128)(2,1)}, u32[]{:S(2)}, u32[]{:S(2)}) %all-to-all-start) | async-done | bytes 1048608 | tf_op jit(solution)/shard_map/cond/branch_1_fun/all_to_all | solution.py:82
  115.1 1.5 reduce_sum.30
  116.6 0.7 pad_maximum_fusion
  117.4 0.0 collective-permute-done
  117.4 1.3 fusion.1
  118.7 3.4 %all-to-all-start.1 = ((bf16[8,128,128]{2,1,0:T(8,128)(2,1)}), bf16[8,128,128]{2,1,0:T(8,128)(2,1)S(1)}, u32[]{:S(2)}, u32[]{:S(2)}) async-start(bf16[8,128,128]{2,1,0:T(8,128)(2,1)} %bitcast.15), calls=%async_computation.1 | async-start | bytes 524288 | tf_op jit(solution)/shard_map/cond/branch_1_fun/all_to_all | solution.py:82
  122.2 2.2 %collective-permute-start.3 = (bf16[128,896]{1,0:T(8,128)(2,1)S(1)}, bf16[128,896]{1,0:T(8,128)(2,1)S(1)}, u32[]{:S(2)}, u32[]{:S(2)}) collective-permute-start(bf16[128,896]{1,0:T(8,128)(2,1)S(1)} %get-tuple-element.45), channel_id=1, source_target_pairs={{128,0},{144,16},{160,32},{176,48},{192,64},{208,80},{224,96},{240... | collective-permute-start | bytes 688136 | tf_op jit(solution)/shard_map/cond/branch_1_fun/ppermute | solution.py:69
  124.4 3.2 %collective-permute-start.2 = (bf16[128,896]{1,0:T(8,128)(2,1)S(1)}, bf16[128,896]{1,0:T(8,128)(2,1)S(1)}, u32[]{:S(2)}, u32[]{:S(2)}) collective-permute-start(bf16[128,896]{1,0:T(8,128)(2,1)S(1)} %get-tuple-element.44), channel_id=1, source_target_pairs={{256,0},{272,16},{288,32},{304,48},{320,64},{336,80},{352,96},{368... | collective-permute-start | bytes 688136 | tf_op jit(solution)/shard_map/cond/branch_1_fun/ppermute | solution.py:69
  127.6 3.6 %collective-permute-start.1 = (bf16[128,896]{1,0:T(8,128)(2,1)S(1)}, bf16[128,896]{1,0:T(8,128)(2,1)}, u32[]{:S(2)}, u32[]{:S(2)}) collective-permute-start(bf16[128,896]{1,0:T(8,128)(2,1)S(1)} %get-tuple-element.43), channel_id=1, source_target_pairs={{384,0},{400,16},{416,32},{432,48},{448,64},{464,80},{480,96},{496... | collective-permute-start | bytes 688136 | tf_op jit(solution)/shard_map/cond/branch_1_fun/ppermute | solution.py:69
  131.2 13.1 %all-to-all-done.1 = bf16[8,128,128]{2,1,0:T(8,128)(2,1)S(1)} async-done(((bf16[8,128,128]{2,1,0:T(8,128)(2,1)}), bf16[8,128,128]{2,1,0:T(8,128)(2,1)S(1)}, u32[]{:S(2)}, u32[]{:S(2)}) %all-to-all-start.1) | async-done | bytes 262176 | tf_op jit(solution)/shard_map/cond/branch_1_fun/all_to_all | solution.py:82
  144.4 4.7 %collective-permute-start.4 = (bf16[128,256]{1,0:T(8,128)(2,1)S(1)}, bf16[128,256]{1,0:T(8,128)(2,1)}, u32[]{:S(2)}, u32[]{:S(2)}) collective-permute-start(bf16[128,256]{1,0:T(8,128)(2,1)S(1)} %pad_maximum_fusion.1), channel_id=1, source_target_pairs={{0,0},{1,1},{2,2},{3,3},{128,4},{129,5},{130,6},{131,7},{256,8},{2... | collective-permute-start | bytes 196616 | tf_op jit(solution)/shard_map/cond/branch_1_fun/ppermute | solution.py:73
  149.0 0.0 collective-permute-done.3
  149.0 0.0 collective-permute-done.2
  149.0 0.0 collective-permute-done.1
  149.1 1.2 fusion.6
  150.3 5.1 %collective-permute-done.4 = bf16[128,256]{1,0:T(8,128)(2,1)} collective-permute-done((bf16[128,256]{1,0:T(8,128)(2,1)S(1)}, bf16[128,256]{1,0:T(8,128)(2,1)}, u32[]{:S(2)}, u32[]{:S(2)}) %collective-permute-start.4) | collective-permute-done | bytes 65568 | tf_op jit(solution)/shard_map/cond/branch_1_fun/ppermute | solution.py:73
  155.3 0.7 multiply_convert_fusion
  156.1 0.0 reduce-scatter.2.cloned.1.call-done
  156.1 1.7 %convert_multiply_fusion = f32[128,896]{1,0:T(8,128)} fusion(bf16[128,896]{1,0:T(8,128)(2,1)} %reduce-scatter.2.cloned.1.call-done), kind=kLoop, calls=%fused_computation.24 | loop fusion | flops 229376 | bytes 688128 | tf_op jit(solution)/shard_map/mul | solution.py:153
  157.8 1.5 copy.18
  (11 shorter events, 0.3 us)
Async XLA Ops:
  7.2 6.0 %copy-start.1 = (bf16[128,256]{1,0:T(8,128)(2,1)S(1)}, bf16[128,256]{1,0:T(8,128)(2,1)}, u32[]{:S(2)}) copy-start(bf16[128,256]{1,0:T(8,128)(2,1)} %param.6) | copy-start | bytes 196612
  7.2 80.5 %all-gather.2.cloned.1.call-start = ((), (), s32[]{:S(2)}) async-start(), calls=%async_computation.5 | async-start | bytes 2293760 | tf_op jit(solution)/shard_map/all_gather | solution.py:129
  9.0 3.4 %collective-permute-start.5 = (bf16[128,896]{1,0:T(8,128)(2,1)S(1)}, bf16[128,896]{1,0:T(8,128)(2,1)S(1)}, u32[]{:S(2)}, u32[]{:S(2)}) collective-permute-start(bf16[128,896]{1,0:T(8,128)(2,1)S(1)} %multiply_convert_fusion.1), channel_id=1, source_target_pairs={{16,0},{0,16},{48,32},{32,48},{80,64},{64,80},{112,96},{96,112},{1... | collective-permute-start | bytes 688136 | tf_op jit(solution)/shard_map/ppermute | solution.py:65
  13.2 10.9 %collective-permute-start.6 = (bf16[128,256]{1,0:T(8,128)(2,1)S(1)}, bf16[128,256]{1,0:T(8,128)(2,1)S(1)}, u32[]{:S(2)}, u32[]{:S(2)}) collective-permute-start(bf16[128,256]{1,0:T(8,128)(2,1)S(1)} %copy-done.1), channel_id=1, source_target_pairs={{0,0},{1,1},{2,2},{3,3},{128,4},{129,5},{130,6},{131,7},{256,8},{2... | collective-permute-start | bytes 196616 | tf_op jit(solution)/shard_map/ppermute | solution.py:73
  24.9 15.6 %all-to-all-start.2 = ((bf16[8,128,128]{2,1,0:T(8,128)(2,1)}), bf16[8,128,128]{2,1,0:T(8,128)(2,1)S(1)}, u32[]{:S(2)}, u32[]{:S(2)}) async-start(bf16[8,128,128]{2,1,0:T(8,128)(2,1)} %bitcast.21), calls=%async_computation.2 | async-start | bytes 524288 | tf_op jit(solution)/shard_map/all_to_all | solution.py:82
  40.6 4.7 %copy-start = (bf16[128,896]{1,0:T(8,128)(2,1)S(1)}, bf16[128,896]{1,0:T(8,128)(2,1)}, u32[]{:S(2)}) copy-start(bf16[128,896]{1,0:T(8,128)(2,1)} %param.7) | copy-start | bytes 688132
  41.7 46.0 %all-to-all-start.3 = ((bf16[4,2,128,512]{3,2,1,0:T(8,128)(2,1)}), bf16[4,2,128,512]{3,2,1,0:T(8,128)(2,1)S(1)}, u32[]{:S(2)}, u32[]{:S(2)}) async-start(bf16[4,2,128,512]{3,2,1,0:T(8,128)(2,1)} %broadcast_in_dim.5), calls=%async_computation.3 | async-start | bytes 2097152 | tf_op jit(solution)/shard_map/all_to_all | solution.py:82
  45.2 110.8 %reduce-scatter.2.cloned.1.call-start = ((), (), s32[]{:S(2)}) async-start(), calls=%async_computation.6 | async-start | bytes 1146880 | tf_op jit(solution)/shard_map/reduce_scatter | solution.py:149
  95.2 19.8 %all-to-all-start = ((bf16[4,2,128,512]{3,2,1,0:T(8,128)(2,1)}), bf16[4,2,128,512]{3,2,1,0:T(8,128)(2,1)}, u32[]{:S(2)}, u32[]{:S(2)}) async-start(bf16[4,2,128,512]{3,2,1,0:T(8,128)(2,1)} %bitcast.10), calls=%async_computation | async-start | bytes 2097152 | tf_op jit(solution)/shard_map/cond/branch_1_fun/all_to_all | solution.py:82
  101.2 16.1 %collective-permute-start = (bf16[4,128,896]{2,1,0:T(8,128)(2,1)S(1)}, bf16[4,128,896]{2,1,0:T(8,128)(2,1)}, u32[]{:S(2)}, u32[]{:S(2)}) collective-permute-start(bf16[4,128,896]{2,1,0:T(8,128)(2,1)S(1)} %fusion), channel_id=1, source_target_pairs={{16,0},{0,16},{48,32},{32,48},{80,64},{64,80},{112,96},{96,112},{1... | collective-permute-start | bytes 2752520 | tf_op jit(solution)/shard_map/cond/branch_1_fun/ppermute | solution.py:65
  118.7 25.6 %all-to-all-start.1 = ((bf16[8,128,128]{2,1,0:T(8,128)(2,1)}), bf16[8,128,128]{2,1,0:T(8,128)(2,1)S(1)}, u32[]{:S(2)}, u32[]{:S(2)}) async-start(bf16[8,128,128]{2,1,0:T(8,128)(2,1)} %bitcast.15), calls=%async_computation.1 | async-start | bytes 524288 | tf_op jit(solution)/shard_map/cond/branch_1_fun/all_to_all | solution.py:82
  122.2 26.9 %collective-permute-start.3 = (bf16[128,896]{1,0:T(8,128)(2,1)S(1)}, bf16[128,896]{1,0:T(8,128)(2,1)S(1)}, u32[]{:S(2)}, u32[]{:S(2)}) collective-permute-start(bf16[128,896]{1,0:T(8,128)(2,1)S(1)} %get-tuple-element.45), channel_id=1, source_target_pairs={{128,0},{144,16},{160,32},{176,48},{192,64},{208,80},{224,96},{240... | collective-permute-start | bytes 688136 | tf_op jit(solution)/shard_map/cond/branch_1_fun/ppermute | solution.py:69
  124.4 24.6 %collective-permute-start.2 = (bf16[128,896]{1,0:T(8,128)(2,1)S(1)}, bf16[128,896]{1,0:T(8,128)(2,1)S(1)}, u32[]{:S(2)}, u32[]{:S(2)}) collective-permute-start(bf16[128,896]{1,0:T(8,128)(2,1)S(1)} %get-tuple-element.44), channel_id=1, source_target_pairs={{256,0},{272,16},{288,32},{304,48},{320,64},{336,80},{352,96},{368... | collective-permute-start | bytes 688136 | tf_op jit(solution)/shard_map/cond/branch_1_fun/ppermute | solution.py:69
  127.6 21.5 %collective-permute-start.1 = (bf16[128,896]{1,0:T(8,128)(2,1)S(1)}, bf16[128,896]{1,0:T(8,128)(2,1)}, u32[]{:S(2)}, u32[]{:S(2)}) collective-permute-start(bf16[128,896]{1,0:T(8,128)(2,1)S(1)} %get-tuple-element.43), channel_id=1, source_target_pairs={{384,0},{400,16},{416,32},{432,48},{448,64},{464,80},{480,96},{496... | collective-permute-start | bytes 688136 | tf_op jit(solution)/shard_map/cond/branch_1_fun/ppermute | solution.py:69
  144.4 11.0 %collective-permute-start.4 = (bf16[128,256]{1,0:T(8,128)(2,1)S(1)}, bf16[128,256]{1,0:T(8,128)(2,1)}, u32[]{:S(2)}, u32[]{:S(2)}) collective-permute-start(bf16[128,256]{1,0:T(8,128)(2,1)S(1)} %pad_maximum_fusion.1), channel_id=1, source_target_pairs={{0,0},{1,1},{2,2},{3,3},{128,4},{129,5},{130,6},{131,7},{256,8},{2... | collective-permute-start | bytes 196616 | tf_op jit(solution)/shard_map/cond/branch_1_fun/ppermute | solution.py:73
Sparse Core Ops, SparseCore 0:
  13.3 39.0 all-gather.1
  91.6 54.3 reduce-scatter.1
where the time goes:
time: 167 us; the launch traced here: 166 us
  waiting for transfers between devices  47.2 us (28%)
  blocking collectives  42.4 us (25%)
  starting transfers between devices  39.9 us (24%)
  between operations  14.1 us (8%)
  other arithmetic  9.94 us (6%)
  matrix products  8.72 us (5%)
  local copies, waits for them, and re-layouts  3.63 us (2%)
    all_gather x1, blocking collectives, on_device(): lax.all_gather(weight, 'dp', axis=0, axis_index_groups=groups_z(), tiled=...  42.4 us
    all_to_all x4, waiting for transfers between devices, exchange(): lax.all_to_all(parts, axis, 0, 0, axis_index_groups=groups, tiled=True)  34.6 us
    all_to_all x4, starting transfers between devices, exchange(): lax.all_to_all(parts, axis, 0, 0, axis_index_groups=groups, tiled=True)  17.5 us
    ppermute x2, waiting for transfers between devices, swap(): return lax.ppermute(block, ('dp', 'tensor'), swap_pairs())  11.1 us
    ppermute x2, starting transfers between devices, swap(): return lax.ppermute(block, ('dp', 'tensor'), swap_pairs())  9.49 us
    ppermute x3, starting transfers between devices, from_x(): return lax.ppermute(block, 'dp', dp_pairs(shift, 0))  8.99 us
    ppermute x2, starting transfers between devices, from_core(): return lax.ppermute(block, 'dp', dp_pairs(0, 1))  3.84 us
    dot_general x1, matrix products, sums(): lax.dot_general(scaled_all, weight_line, (((1,), (1,)), ((), ())), prefer...  3.76 us
  transfers between devices with their start and end apart: 13, of which 6 were waited for; matrix products, arithmetic and copies ran while one was open for 8% of the time, Pallas kernels for 0%

commit v1 on v0

--- a/solution.py
+++ b/solution.py
@@ -124,11 +124,8 @@
     col_scale = jnp.sum(membership * level_vals[:, None], axis=0)
 
     scaled = (cotangent.astype(wide) * col_scale[None, :]).astype(narrow)
+    both = ("dp", "tensor")
     scaled_pair = jnp.concatenate([scaled, from_core(scaled)], axis=0)
-    scaled_pair, tokens = lax.optimization_barrier((scaled_pair, tokens))
-    scaled_all = lax.all_gather(scaled_pair, "dp", axis=0, axis_index_groups=groups_x(), tiled=True)
-
-    both = ("dp", "tensor")
 
     crossed = swap(tokens)
     parts = jnp.stack([crossed[:, :half], crossed[:, half:]])
@@ -137,8 +134,10 @@
     line = line.reshape(RING, 2, token_rows, half)
     line = jnp.concatenate([line[i] for i in range(RING)], axis=2)
     line = near_first(line, core)
-    line, weight = lax.optimization_barrier((line, weight))
+    line, weight, scaled_pair = lax.optimization_barrier((line, weight, scaled_pair))
     brick = collect(line, "tensor", groups_y()).reshape(-1, RING * half)
+
+    scaled_all = lax.all_gather(scaled_pair, "dp", axis=0, axis_index_groups=groups_x(), tiled=True)
 
     weight_line = lax.all_gather(weight, "dp", axis=0, axis_index_groups=groups_z(), tiled=True)
     brick, weight_line = lax.optimization_barrier((brick, weight_line))

time: 167 us -> 161 us (0.964)
  waiting for transfers between devices: 47.2 us -> 38.7 us
  starting transfers between devices: 39.9 us -> 42.5 us
    all_to_all x4, waiting for transfers between devices: 34.6 us -> 26.2 us  [exchange(): lax.all_to_all(parts, axis, 0, 0, axis_index_groups=groups, tiled=True)]
  transfers between devices with their start and end apart: 13 -> 13, of which waited for: 6 -> 6; matrix products, arithmetic and copies ran while one was open for 8% -> 9% of each run, Pallas kernels for 0% -> 0%
where the time goes in v1:
time: 161 us; the launch traced here: 160 us
  starting transfers between devices  42.5 us (26%)
  blocking collectives  42.2 us (26%)
  waiting for transfers between devices  38.7 us (24%)
  between operations  14.1 us (9%)
  other arithmetic  9.94 us (6%)
  matrix products  8.72 us (5%)
  local copies, waits for them, and re-layouts  3.58 us (2%)
    all_gather x1, blocking collectives, on_device(): lax.all_gather(weight, 'dp', axis=0, axis_index_groups=groups_z(), tiled=...  42.2 us
    all_to_all x4, waiting for transfers between devices, exchange(): lax.all_to_all(parts, axis, 0, 0, axis_index_groups=groups, tiled=True)  26.2 us
    all_to_all x4, starting transfers between devices, exchange(): lax.all_to_all(parts, axis, 0, 0, axis_index_groups=groups, tiled=True)  18 us
    ppermute x2, waiting for transfers between devices, swap(): return lax.ppermute(block, ('dp', 'tensor'), swap_pairs())  11.3 us
    ppermute x3, starting transfers between devices, from_x(): return lax.ppermute(block, 'dp', dp_pairs(shift, 0))  10.6 us
    ppermute x2, starting transfers between devices, swap(): return lax.ppermute(block, ('dp', 'tensor'), swap_pairs())  9.48 us
    ppermute x2, starting transfers between devices, from_core(): return lax.ppermute(block, 'dp', dp_pairs(0, 1))  4.29 us
    dot_general x1, matrix products, sums(): lax.dot_general(scaled_all, weight_line, (((1,), (1,)), ((), ())), prefer...  3.76 us
  transfers between devices with their start and end apart: 13, of which 6 were waited for; matrix products, arithmetic and copies ran while one was open for 9% of the time, Pallas kernels for 0%

profile of v1, /device:TPU:6, one launch (start us, length us, event | category | flops | bytes accessed | tf_op | source)
XLA Modules:
  0.0 160.1 jit_solution(7156269605176926663)
XLA Ops:
  7.2 4.8 %collective-permute-start.5 = (bf16[128,256]{1,0:T(8,128)(2,1)}, bf16[128,256]{1,0:T(8,128)(2,1)S(1)}, u32[]{:S(2)}, u32[]{:S(2)}) collective-permute-start(bf16[128,256]{1,0:T(8,128)(2,1)} %param.6), channel_id=1, source_target_pairs={{0,0},{1,1},{2,2},{3,3},{128,4},{129,5},{130,6},{131,7},{256,8},{2... | collective-permute-start | bytes 196616 | tf_op jit(solution)/shard_map/ppermute | solution.py:73
  12.0 6.2 %collective-permute-done.5 = bf16[128,256]{1,0:T(8,128)(2,1)S(1)} collective-permute-done((bf16[128,256]{1,0:T(8,128)(2,1)}, bf16[128,256]{1,0:T(8,128)(2,1)S(1)}, u32[]{:S(2)}, u32[]{:S(2)}) %collective-permute-start.5) | collective-permute-done | bytes 65568 | tf_op jit(solution)/shard_map/ppermute | solution.py:73
  18.3 0.7 broadcast_in_dim.4
  19.0 5.9 %all-to-all-start.2 = ((bf16[8,128,128]{2,1,0:T(8,128)(2,1)}), bf16[8,128,128]{2,1,0:T(8,128)(2,1)S(1)}, u32[]{:S(2)}, u32[]{:S(2)}) async-start(bf16[8,128,128]{2,1,0:T(8,128)(2,1)} %bitcast.21), calls=%async_computation.2 | async-start | bytes 524288 | tf_op jit(solution)/shard_map/all_to_all | solution.py:82
  24.9 0.0 all-gather.2.cloned.1.call-start
  24.9 0.7 convert_multiply_fusion.1
  25.6 0.1 select_reduce_fusion
  25.7 1.0 multiply_convert_fusion.1
  26.7 2.4 %collective-permute-start.6 = (bf16[128,896]{1,0:T(8,128)(2,1)S(1)}, bf16[128,896]{1,0:T(8,128)(2,1)S(1)}, u32[]{:S(2)}, u32[]{:S(2)}) collective-permute-start(bf16[128,896]{1,0:T(8,128)(2,1)S(1)} %multiply_convert_fusion.1), channel_id=1, source_target_pairs={{16,0},{0,16},{48,32},{32,48},{80,64},{64,80},{112,96},{96,112},{1... | collective-permute-start | bytes 688136 | tf_op jit(solution)/shard_map/ppermute | solution.py:65
  29.1 1.1 collective-permute-done.6
  30.2 0.8 pad_maximum_fusion.2
  31.0 3.7 %all-to-all-done.2 = bf16[8,128,128]{2,1,0:T(8,128)(2,1)S(1)} async-done(((bf16[8,128,128]{2,1,0:T(8,128)(2,1)}), bf16[8,128,128]{2,1,0:T(8,128)(2,1)S(1)}, u32[]{:S(2)}, u32[]{:S(2)}) %all-to-all-start.2) | async-done | bytes 262176 | tf_op jit(solution)/shard_map/all_to_all | solution.py:82
  34.8 0.0 copy-start
  34.8 0.0 all-gather.2.cloned.1.call-update
  34.8 1.1 broadcast_in_dim.5
  35.9 3.5 %all-to-all-start.3 = ((bf16[4,2,128,512]{3,2,1,0:T(8,128)(2,1)}), bf16[4,2,128,512]{3,2,1,0:T(8,128)(2,1)S(1)}, u32[]{:S(2)}, u32[]{:S(2)}) async-start(bf16[4,2,128,512]{3,2,1,0:T(8,128)(2,1)} %broadcast_in_dim.5), calls=%async_computation.3 | async-start | bytes 2097152 | tf_op jit(solution)/shard_map/all_to_all | solution.py:82
  39.4 0.0 reduce-scatter.2.cloned.1.call-start
  39.5 0.0 copy-done
  39.5 42.2 %all_gather.6 = bf16[512,896]{1,0:T(8,128)(2,1)S(1)} all-gather(bf16[128,896]{1,0:T(8,128)(2,1)S(1)} %copy-done), channel_id=1, replica_groups={{0,32,64,96},{16,48,80,112},{128,160,192,224},{144,176,208,240},{256,28..., dimensions={0}, use_global_device_ids=true | all-gather | bytes 1146880 | tf_op jit(solution)/shard_map/all_gather | solution.py:142
  81.7 0.0 all-to-all-done.3
  81.7 0.0 all-gather.2.cloned.1.call-done
  81.7 3.7 %convolution_convert_fusion.1 = bf16[512,896]{1,0:T(8,128)(2,1)} fusion(bf16[1024,512]{1,0:T(8,128)(2,1)S(1)} %bitcast.52, bf16[1024,896]{1,0:T(8,128)(2,1)} %all-gather.2.cloned.1.call-done), kind=kOutput, calls=%fused_computation.22 | convolution fusion | flops 939982848 | bytes 3801088 | tf_op jit(solution)/shard_map/dot_general | solution.py:145
  85.4 0.0 reduce-scatter.2.cloned.1.call-update
  85.5 63.8 %conditional.1 = (f32[128,896]{1,0:T(8,128)S(1)}, bf16[128,256]{1,0:T(8,128)(2,1)}) conditional(s32[]{:T(128)} %convert_element_type.75, () %tuple.22, (bf16[1024,512]{1,0:T(8,128)(2,1)S(1)}, bf16[512,896]{1,0:T(8,128)(2,1)S(1)}, s32[]{:T(128)}, s32[]{:T(128)}, pred[]{:T(512)}, /*index=5*/s32[]{:T(128)}, bf16[1024,896]{1,0:T(8,128)(2,1)}) %tuple.46), branch_computations={%region_1.2_spmd, %region_2.5_spmd} | conditional | flops 1882669056 | bytes 33621000 | solution.py:99
  85.5 3.8 %convolution_convert_fusion = bf16[1024,512]{1,0:T(8,128)(2,1)} fusion(bf16[1024,896]{1,0:T(8,128)(2,1)} %get-tuple-element.42, bf16[512,896]{1,0:T(8,128)(2,1)S(1)} %get-tuple-element.37), kind=kOutput, calls=%fused_computation.1 | convolution fusion | flops 940048384 | bytes 3801088 | tf_op jit(solution)/shard_map/cond/branch_1_fun/dot_general | solution.py:155
  89.2 5.2 %all-to-all-start = ((bf16[4,2,128,512]{3,2,1,0:T(8,128)(2,1)}), bf16[4,2,128,512]{3,2,1,0:T(8,128)(2,1)}, u32[]{:S(2)}, u32[]{:S(2)}) async-start(bf16[4,2,128,512]{3,2,1,0:T(8,128)(2,1)} %bitcast.10), calls=%async_computation | async-start | bytes 2097152 | tf_op jit(solution)/shard_map/cond/branch_1_fun/all_to_all | solution.py:82
  94.4 1.2 fusion.11
  95.7 0.1 fusion
  95.8 1.9 %collective-permute-start = (bf16[4,128,896]{2,1,0:T(8,128)(2,1)S(1)}, bf16[4,128,896]{2,1,0:T(8,128)(2,1)}, u32[]{:S(2)}, u32[]{:S(2)}) collective-permute-start(bf16[4,128,896]{2,1,0:T(8,128)(2,1)S(1)} %fusion), channel_id=1, source_target_pairs={{16,0},{0,16},{48,32},{32,48},{80,64},{64,80},{112,96},{96,112},{1... | collective-permute-start | bytes 2752520 | tf_op jit(solution)/shard_map/cond/branch_1_fun/ppermute | solution.py:65
  97.7 0.1 slice.56
  97.9 11.0 %all-to-all-done = bf16[4,2,128,512]{3,2,1,0:T(8,128)(2,1)} async-done(((bf16[4,2,128,512]{3,2,1,0:T(8,128)(2,1)}), bf16[4,2,128,512]{3,2,1,0:T(8,128)(2,1)}, u32[]{:S(2)}, u32[]{:S(2)}) %all-to-all-start) | async-done | bytes 1048608 | tf_op jit(solution)/shard_map/cond/branch_1_fun/all_to_all | solution.py:82
  108.9 1.5 reduce_sum.30
  110.5 0.7 pad_maximum_fusion
  111.2 0.0 collective-permute-done
  111.2 1.3 fusion.1
  112.6 3.4 %all-to-all-start.1 = ((bf16[8,128,128]{2,1,0:T(8,128)(2,1)}), bf16[8,128,128]{2,1,0:T(8,128)(2,1)S(1)}, u32[]{:S(2)}, u32[]{:S(2)}) async-start(bf16[8,128,128]{2,1,0:T(8,128)(2,1)} %bitcast.15), calls=%async_computation.1 | async-start | bytes 524288 | tf_op jit(solution)/shard_map/cond/branch_1_fun/all_to_all | solution.py:82
  116.0 2.3 %collective-permute-start.3 = (bf16[128,896]{1,0:T(8,128)(2,1)S(1)}, bf16[128,896]{1,0:T(8,128)(2,1)S(1)}, u32[]{:S(2)}, u32[]{:S(2)}) collective-permute-start(bf16[128,896]{1,0:T(8,128)(2,1)S(1)} %get-tuple-element.45), channel_id=1, source_target_pairs={{128,0},{144,16},{160,32},{176,48},{192,64},{208,80},{224,96},{240... | collective-permute-start | bytes 688136 | tf_op jit(solution)/shard_map/cond/branch_1_fun/ppermute | solution.py:69
  118.4 4.7 %collective-permute-start.2 = (bf16[128,896]{1,0:T(8,128)(2,1)S(1)}, bf16[128,896]{1,0:T(8,128)(2,1)S(1)}, u32[]{:S(2)}, u32[]{:S(2)}) collective-permute-start(bf16[128,896]{1,0:T(8,128)(2,1)S(1)} %get-tuple-element.44), channel_id=1, source_target_pairs={{256,0},{272,16},{288,32},{304,48},{320,64},{336,80},{352,96},{368... | collective-permute-start | bytes 688136 | tf_op jit(solution)/shard_map/cond/branch_1_fun/ppermute | solution.py:69
  123.1 3.6 %collective-permute-start.1 = (bf16[128,896]{1,0:T(8,128)(2,1)S(1)}, bf16[128,896]{1,0:T(8,128)(2,1)}, u32[]{:S(2)}, u32[]{:S(2)}) collective-permute-start(bf16[128,896]{1,0:T(8,128)(2,1)S(1)} %get-tuple-element.43), channel_id=1, source_target_pairs={{384,0},{400,16},{416,32},{432,48},{448,64},{464,80},{480,96},{496... | collective-permute-start | bytes 688136 | tf_op jit(solution)/shard_map/cond/branch_1_fun/ppermute | solution.py:69
  126.7 11.5 %all-to-all-done.1 = bf16[8,128,128]{2,1,0:T(8,128)(2,1)S(1)} async-done(((bf16[8,128,128]{2,1,0:T(8,128)(2,1)}), bf16[8,128,128]{2,1,0:T(8,128)(2,1)S(1)}, u32[]{:S(2)}, u32[]{:S(2)}) %all-to-all-start.1) | async-done | bytes 262176 | tf_op jit(solution)/shard_map/cond/branch_1_fun/all_to_all | solution.py:82
  138.3 4.6 %collective-permute-start.4 = (bf16[128,256]{1,0:T(8,128)(2,1)S(1)}, bf16[128,256]{1,0:T(8,128)(2,1)}, u32[]{:S(2)}, u32[]{:S(2)}) collective-permute-start(bf16[128,256]{1,0:T(8,128)(2,1)S(1)} %pad_maximum_fusion.1), channel_id=1, source_target_pairs={{0,0},{1,1},{2,2},{3,3},{128,4},{129,5},{130,6},{131,7},{256,8},{2... | collective-permute-start | bytes 196616 | tf_op jit(solution)/shard_map/cond/branch_1_fun/ppermute | solution.py:73
  143.0 0.0 collective-permute-done.3
  143.0 0.0 collective-permute-done.2
  143.0 0.0 collective-permute-done.1
  143.0 1.2 fusion.6
  144.2 5.1 %collective-permute-done.4 = bf16[128,256]{1,0:T(8,128)(2,1)} collective-permute-done((bf16[128,256]{1,0:T(8,128)(2,1)S(1)}, bf16[128,256]{1,0:T(8,128)(2,1)}, u32[]{:S(2)}, u32[]{:S(2)}) %collective-permute-start.4) | collective-permute-done | bytes 65568 | tf_op jit(solution)/shard_map/cond/branch_1_fun/ppermute | solution.py:73
  149.3 0.7 multiply_convert_fusion
  150.0 0.0 reduce-scatter.2.cloned.1.call-done
  150.0 1.7 %convert_multiply_fusion = f32[128,896]{1,0:T(8,128)} fusion(bf16[128,896]{1,0:T(8,128)(2,1)} %reduce-scatter.2.cloned.1.call-done), kind=kLoop, calls=%fused_computation.24 | loop fusion | flops 229376 | bytes 688128 | tf_op jit(solution)/shard_map/mul | solution.py:152
  151.7 1.5 copy.18
  (11 shorter events, 0.3 us)
Async XLA Ops:
  7.2 11.1 %collective-permute-start.5 = (bf16[128,256]{1,0:T(8,128)(2,1)}, bf16[128,256]{1,0:T(8,128)(2,1)S(1)}, u32[]{:S(2)}, u32[]{:S(2)}) collective-permute-start(bf16[128,256]{1,0:T(8,128)(2,1)} %param.6), channel_id=1, source_target_pairs={{0,0},{1,1},{2,2},{3,3},{128,4},{129,5},{130,6},{131,7},{256,8},{2... | collective-permute-start | bytes 196616 | tf_op jit(solution)/shard_map/ppermute | solution.py:73
  19.0 15.6 %all-to-all-start.2 = ((bf16[8,128,128]{2,1,0:T(8,128)(2,1)}), bf16[8,128,128]{2,1,0:T(8,128)(2,1)S(1)}, u32[]{:S(2)}, u32[]{:S(2)}) async-start(bf16[8,128,128]{2,1,0:T(8,128)(2,1)} %bitcast.21), calls=%async_computation.2 | async-start | bytes 524288 | tf_op jit(solution)/shard_map/all_to_all | solution.py:82
  24.9 56.8 %all-gather.2.cloned.1.call-start = ((), (), s32[]{:S(2)}) async-start(), calls=%async_computation.5 | async-start | bytes 2293760 | tf_op jit(solution)/shard_map/all_gather | solution.py:140
  26.7 3.5 %collective-permute-start.6 = (bf16[128,896]{1,0:T(8,128)(2,1)S(1)}, bf16[128,896]{1,0:T(8,128)(2,1)S(1)}, u32[]{:S(2)}, u32[]{:S(2)}) collective-permute-start(bf16[128,896]{1,0:T(8,128)(2,1)S(1)} %multiply_convert_fusion.1), channel_id=1, source_target_pairs={{16,0},{0,16},{48,32},{32,48},{80,64},{64,80},{112,96},{96,112},{1... | collective-permute-start | bytes 688136 | tf_op jit(solution)/shard_map/ppermute | solution.py:65
  34.8 4.7 %copy-start = (bf16[128,896]{1,0:T(8,128)(2,1)S(1)}, bf16[128,896]{1,0:T(8,128)(2,1)}, u32[]{:S(2)}) copy-start(bf16[128,896]{1,0:T(8,128)(2,1)} %param.7) | copy-start | bytes 688132
  35.9 45.8 %all-to-all-start.3 = ((bf16[4,2,128,512]{3,2,1,0:T(8,128)(2,1)}), bf16[4,2,128,512]{3,2,1,0:T(8,128)(2,1)S(1)}, u32[]{:S(2)}, u32[]{:S(2)}) async-start(bf16[4,2,128,512]{3,2,1,0:T(8,128)(2,1)} %broadcast_in_dim.5), calls=%async_computation.3 | async-start | bytes 2097152 | tf_op jit(solution)/shard_map/all_to_all | solution.py:82
  39.4 110.6 %reduce-scatter.2.cloned.1.call-start = ((), (), s32[]{:S(2)}) async-start(), calls=%async_computation.6 | async-start | bytes 1146880 | tf_op jit(solution)/shard_map/reduce_scatter | solution.py:148
  89.2 19.7 %all-to-all-start = ((bf16[4,2,128,512]{3,2,1,0:T(8,128)(2,1)}), bf16[4,2,128,512]{3,2,1,0:T(8,128)(2,1)}, u32[]{:S(2)}, u32[]{:S(2)}) async-start(bf16[4,2,128,512]{3,2,1,0:T(8,128)(2,1)} %bitcast.10), calls=%async_computation | async-start | bytes 2097152 | tf_op jit(solution)/shard_map/cond/branch_1_fun/all_to_all | solution.py:82
  95.8 15.5 %collective-permute-start = (bf16[4,128,896]{2,1,0:T(8,128)(2,1)S(1)}, bf16[4,128,896]{2,1,0:T(8,128)(2,1)}, u32[]{:S(2)}, u32[]{:S(2)}) collective-permute-start(bf16[4,128,896]{2,1,0:T(8,128)(2,1)S(1)} %fusion), channel_id=1, source_target_pairs={{16,0},{0,16},{48,32},{32,48},{80,64},{64,80},{112,96},{96,112},{1... | collective-permute-start | bytes 2752520 | tf_op jit(solution)/shard_map/cond/branch_1_fun/ppermute | solution.py:65
  112.6 25.6 %all-to-all-start.1 = ((bf16[8,128,128]{2,1,0:T(8,128)(2,1)}), bf16[8,128,128]{2,1,0:T(8,128)(2,1)S(1)}, u32[]{:S(2)}, u32[]{:S(2)}) async-start(bf16[8,128,128]{2,1,0:T(8,128)(2,1)} %bitcast.15), calls=%async_computation.1 | async-start | bytes 524288 | tf_op jit(solution)/shard_map/cond/branch_1_fun/all_to_all | solution.py:82
  116.0 26.9 %collective-permute-start.3 = (bf16[128,896]{1,0:T(8,128)(2,1)S(1)}, bf16[128,896]{1,0:T(8,128)(2,1)S(1)}, u32[]{:S(2)}, u32[]{:S(2)}) collective-permute-start(bf16[128,896]{1,0:T(8,128)(2,1)S(1)} %get-tuple-element.45), channel_id=1, source_target_pairs={{128,0},{144,16},{160,32},{176,48},{192,64},{208,80},{224,96},{240... | collective-permute-start | bytes 688136 | tf_op jit(solution)/shard_map/cond/branch_1_fun/ppermute | solution.py:69
  118.4 24.6 %collective-permute-start.2 = (bf16[128,896]{1,0:T(8,128)(2,1)S(1)}, bf16[128,896]{1,0:T(8,128)(2,1)S(1)}, u32[]{:S(2)}, u32[]{:S(2)}) collective-permute-start(bf16[128,896]{1,0:T(8,128)(2,1)S(1)} %get-tuple-element.44), channel_id=1, source_target_pairs={{256,0},{272,16},{288,32},{304,48},{320,64},{336,80},{352,96},{368... | collective-permute-start | bytes 688136 | tf_op jit(solution)/shard_map/cond/branch_1_fun/ppermute | solution.py:69
  123.1 19.9 %collective-permute-start.1 = (bf16[128,896]{1,0:T(8,128)(2,1)S(1)}, bf16[128,896]{1,0:T(8,128)(2,1)}, u32[]{:S(2)}, u32[]{:S(2)}) collective-permute-start(bf16[128,896]{1,0:T(8,128)(2,1)S(1)} %get-tuple-element.43), channel_id=1, source_target_pairs={{384,0},{400,16},{416,32},{432,48},{448,64},{464,80},{480,96},{496... | collective-permute-start | bytes 688136 | tf_op jit(solution)/shard_map/cond/branch_1_fun/ppermute | solution.py:69
  138.3 11.0 %collective-permute-start.4 = (bf16[128,256]{1,0:T(8,128)(2,1)S(1)}, bf16[128,256]{1,0:T(8,128)(2,1)}, u32[]{:S(2)}, u32[]{:S(2)}) collective-permute-start(bf16[128,256]{1,0:T(8,128)(2,1)S(1)} %pad_maximum_fusion.1), channel_id=1, source_target_pairs={{0,0},{1,1},{2,2},{3,3},{128,4},{129,5},{130,6},{131,7},{256,8},{2... | collective-permute-start | bytes 196616 | tf_op jit(solution)/shard_map/cond/branch_1_fun/ppermute | solution.py:73
Sparse Core Ops, SparseCore 0:
  34.9 33.9 all-gather.1
  85.6 54.1 reduce-scatter.1

commit v2 on v1

--- a/solution.py
+++ b/solution.py
@@ -174,10 +174,11 @@
 
         term = exchange(term.reshape(2 * RING, token_rows, half), both, groups_core_low())
         term = total(term.reshape(RING, 2, token_rows, half)).astype(narrow)
-        input_grad = swap(jnp.concatenate([term[0], term[1]], axis=1))
-        return running, input_grad
+        term = jnp.concatenate([term[0], term[1]], axis=1)
+        return running, term
 
-    running, input_grad = block_of(sums, dp, scaled_all, brick, weight_line)
+    running, term = block_of(sums, dp, scaled_all, brick, weight_line)
+    input_grad = swap(term)
     output = (running * col_scale[None, :]).astype(narrow)
     return (output, input_grad, weight_grad)
 

time: 161 us -> 159 us (0.988)
    all_to_all x4, waiting for transfers between devices: 26.2 us -> 17.4 us  [exchange(): lax.all_to_all(parts, axis, 0, 0, axis_index_groups=groups, tiled=True)]
    ppermute x3, waiting for transfers between devices: 0.01 us -> 7.72 us  [from_x(): return lax.ppermute(block, 'dp', dp_pairs(shift, 0))]
  transfers between devices with their start and end apart: 13 -> 13, of which waited for: 6 -> 9; matrix products, arithmetic and copies ran while one was open for 9% -> 9% of each run, Pallas kernels for 0% -> 0%
where the time goes in v2:
time: 159 us; the launch traced here: 158 us
  starting transfers between devices  42.5 us (27%)
  blocking collectives  42.2 us (27%)
  waiting for transfers between devices  38 us (24%)
  between operations  14.2 us (9%)
  other arithmetic  9.81 us (6%)
  matrix products  8.72 us (5%)
  local copies, waits for them, and re-layouts  2.74 us (2%)
    all_gather x1, blocking collectives, on_device(): lax.all_gather(weight, 'dp', axis=0, axis_index_groups=groups_z(), tiled=...  42.2 us
    all_to_all x4, starting transfers between devices, exchange(): lax.all_to_all(parts, axis, 0, 0, axis_index_groups=groups, tiled=True)  18 us
    all_to_all x4, waiting for transfers between devices, exchange(): lax.all_to_all(parts, axis, 0, 0, axis_index_groups=groups, tiled=True)  17.4 us
    ppermute x2, waiting for transfers between devices, swap(): return lax.ppermute(block, ('dp', 'tensor'), swap_pairs())  11.7 us
    ppermute x3, starting transfers between devices, from_x(): return lax.ppermute(block, 'dp', dp_pairs(shift, 0))  10.6 us
    ppermute x2, starting transfers between devices, swap(): return lax.ppermute(block, ('dp', 'tensor'), swap_pairs())  9.48 us
    ppermute x3, waiting for transfers between devices, from_x(): return lax.ppermute(block, 'dp', dp_pairs(shift, 0))  7.72 us
    ppermute x2, starting transfers between devices, from_core(): return lax.ppermute(block, 'dp', dp_pairs(0, 1))  4.29 us
  transfers between devices with their start and end apart: 13, of which 9 were waited for; matrix products, arithmetic and copies ran while one was open for 9% of the time, Pallas kernels for 0%

profile of v2, /device:TPU:6, one launch (start us, length us, event | category | flops | bytes accessed | tf_op | source)
XLA Modules:
  0.0 158.4 jit_solution(17811871366855320015)
XLA Ops:
  7.2 4.8 %collective-permute-start.4 = (bf16[128,256]{1,0:T(8,128)(2,1)}, bf16[128,256]{1,0:T(8,128)(2,1)S(1)}, u32[]{:S(2)}, u32[]{:S(2)}) collective-permute-start(bf16[128,256]{1,0:T(8,128)(2,1)} %param.6), channel_id=1, source_target_pairs={{0,0},{1,1},{2,2},{3,3},{128,4},{129,5},{130,6},{131,7},{256,8},{2... | collective-permute-start | bytes 196616 | tf_op jit(solution)/shard_map/ppermute | solution.py:73
  12.0 6.2 %collective-permute-done.4 = bf16[128,256]{1,0:T(8,128)(2,1)S(1)} collective-permute-done((bf16[128,256]{1,0:T(8,128)(2,1)}, bf16[128,256]{1,0:T(8,128)(2,1)S(1)}, u32[]{:S(2)}, u32[]{:S(2)}) %collective-permute-start.4) | collective-permute-done | bytes 65568 | tf_op jit(solution)/shard_map/ppermute | solution.py:73
  18.3 0.7 broadcast_in_dim.4
  19.0 5.9 %all-to-all-start.2 = ((bf16[8,128,128]{2,1,0:T(8,128)(2,1)}), bf16[8,128,128]{2,1,0:T(8,128)(2,1)S(1)}, u32[]{:S(2)}, u32[]{:S(2)}) async-start(bf16[8,128,128]{2,1,0:T(8,128)(2,1)} %bitcast.21), calls=%async_computation.2 | async-start | bytes 524288 | tf_op jit(solution)/shard_map/all_to_all | solution.py:82
  24.9 0.0 all-gather.2.cloned.1.call-start
  24.9 0.7 convert_multiply_fusion.1
  25.6 0.1 select_reduce_fusion
  25.7 1.0 multiply_convert_fusion.1
  26.7 2.4 %collective-permute-start.5 = (bf16[128,896]{1,0:T(8,128)(2,1)S(1)}, bf16[128,896]{1,0:T(8,128)(2,1)S(1)}, u32[]{:S(2)}, u32[]{:S(2)}) collective-permute-start(bf16[128,896]{1,0:T(8,128)(2,1)S(1)} %multiply_convert_fusion.1), channel_id=1, source_target_pairs={{16,0},{0,16},{48,32},{32,48},{80,64},{64,80},{112,96},{96,112},{1... | collective-permute-start | bytes 688136 | tf_op jit(solution)/shard_map/ppermute | solution.py:65
  29.1 1.1 collective-permute-done.5
  30.2 0.8 pad_maximum_fusion.2
  31.0 3.7 %all-to-all-done.2 = bf16[8,128,128]{2,1,0:T(8,128)(2,1)S(1)} async-done(((bf16[8,128,128]{2,1,0:T(8,128)(2,1)}), bf16[8,128,128]{2,1,0:T(8,128)(2,1)S(1)}, u32[]{:S(2)}, u32[]{:S(2)}) %all-to-all-start.2) | async-done | bytes 262176 | tf_op jit(solution)/shard_map/all_to_all | solution.py:82
  34.8 0.0 copy-start
  34.8 0.0 all-gather.2.cloned.1.call-update
  34.8 1.1 broadcast_in_dim.5
  35.9 3.5 %all-to-all-start.3 = ((bf16[4,2,128,512]{3,2,1,0:T(8,128)(2,1)}), bf16[4,2,128,512]{3,2,1,0:T(8,128)(2,1)S(1)}, u32[]{:S(2)}, u32[]{:S(2)}) async-start(bf16[4,2,128,512]{3,2,1,0:T(8,128)(2,1)} %broadcast_in_dim.5), calls=%async_computation.3 | async-start | bytes 2097152 | tf_op jit(solution)/shard_map/all_to_all | solution.py:82
  39.4 0.0 reduce-scatter.2.cloned.1.call-start
  39.5 0.0 copy-done
  39.5 42.2 %all_gather.6 = bf16[512,896]{1,0:T(8,128)(2,1)S(1)} all-gather(bf16[128,896]{1,0:T(8,128)(2,1)S(1)} %copy-done), channel_id=1, replica_groups={{0,32,64,96},{16,48,80,112},{128,160,192,224},{144,176,208,240},{256,28..., dimensions={0}, use_global_device_ids=true | all-gather | bytes 1146880 | tf_op jit(solution)/shard_map/all_gather | solution.py:142
  81.7 0.0 all-to-all-done.3
  81.7 0.0 all-gather.2.cloned.1.call-done
  81.7 3.7 %convolution_convert_fusion.1 = bf16[512,896]{1,0:T(8,128)(2,1)} fusion(bf16[1024,512]{1,0:T(8,128)(2,1)S(1)} %bitcast.52, bf16[1024,896]{1,0:T(8,128)(2,1)} %all-gather.2.cloned.1.call-done), kind=kOutput, calls=%fused_computation.22 | convolution fusion | flops 939982848 | bytes 3801088 | tf_op jit(solution)/shard_map/dot_general | solution.py:145
  85.4 0.0 reduce-scatter.2.cloned.1.call-update
  85.5 52.8 %conditional.1 = (f32[128,896]{1,0:T(8,128)S(1)}, bf16[128,256]{1,0:T(8,128)(2,1)S(1)}) conditional(s32[]{:T(128)} %convert_element_type.75, () %tuple.22, (bf16[1024,512]{1,0:T(8,128)(2,1)S(1)}, bf16[512,896]{1,0:T(8,128)(2,1)S(1)}, s32[]{:T(128)}, s32[]{:T(128)}, pred[]{:T(512)}, /*index=5*/s32[]{:T(128)}, bf16[1024,896]{1,0:T(8,128)(2,1)}) %tuple.46), branch_computations={%region_1.2_spmd, %region_2.5_spmd} | conditional | flops 1882669056 | bytes 33358814 | solution.py:99
  85.5 3.8 %convolution_convert_fusion = bf16[1024,512]{1,0:T(8,128)(2,1)} fusion(bf16[1024,896]{1,0:T(8,128)(2,1)} %get-tuple-element.42, bf16[512,896]{1,0:T(8,128)(2,1)S(1)} %get-tuple-element.37), kind=kOutput, calls=%fused_computation.1 | convolution fusion | flops 940048384 | bytes 3801088 | tf_op jit(solution)/shard_map/cond/branch_1_fun/dot_general | solution.py:155
  89.2 5.2 %all-to-all-start = ((bf16[4,2,128,512]{3,2,1,0:T(8,128)(2,1)}), bf16[4,2,128,512]{3,2,1,0:T(8,128)(2,1)}, u32[]{:S(2)}, u32[]{:S(2)}) async-start(bf16[4,2,128,512]{3,2,1,0:T(8,128)(2,1)} %bitcast.10), calls=%async_computation | async-start | bytes 2097152 | tf_op jit(solution)/shard_map/cond/branch_1_fun/all_to_all | solution.py:82
  94.4 1.2 fusion.11
  95.7 0.1 fusion
  95.8 1.9 %collective-permute-start = (bf16[4,128,896]{2,1,0:T(8,128)(2,1)S(1)}, bf16[4,128,896]{2,1,0:T(8,128)(2,1)}, u32[]{:S(2)}, u32[]{:S(2)}) collective-permute-start(bf16[4,128,896]{2,1,0:T(8,128)(2,1)S(1)} %fusion), channel_id=1, source_target_pairs={{16,0},{0,16},{48,32},{32,48},{80,64},{64,80},{112,96},{96,112},{1... | collective-permute-start | bytes 2752520 | tf_op jit(solution)/shard_map/cond/branch_1_fun/ppermute | solution.py:65
  97.7 0.1 slice.56
  97.9 11.0 %all-to-all-done = bf16[4,2,128,512]{3,2,1,0:T(8,128)(2,1)} async-done(((bf16[4,2,128,512]{3,2,1,0:T(8,128)(2,1)}), bf16[4,2,128,512]{3,2,1,0:T(8,128)(2,1)}, u32[]{:S(2)}, u32[]{:S(2)}) %all-to-all-start) | async-done | bytes 1048608 | tf_op jit(solution)/shard_map/cond/branch_1_fun/all_to_all | solution.py:82
  108.9 1.5 reduce_sum.30
  110.5 0.7 pad_maximum_fusion
  111.2 0.0 collective-permute-done
  111.2 1.3 fusion.1
  112.6 3.4 %all-to-all-start.1 = ((bf16[8,128,128]{2,1,0:T(8,128)(2,1)}), bf16[8,128,128]{2,1,0:T(8,128)(2,1)S(1)}, u32[]{:S(2)}, u32[]{:S(2)}) async-start(bf16[8,128,128]{2,1,0:T(8,128)(2,1)} %bitcast.15), calls=%async_computation.1 | async-start | bytes 524288 | tf_op jit(solution)/shard_map/cond/branch_1_fun/all_to_all | solution.py:82
  116.0 2.4 %collective-permute-start.3 = (bf16[128,896]{1,0:T(8,128)(2,1)S(1)}, bf16[128,896]{1,0:T(8,128)(2,1)S(1)}, u32[]{:S(2)}, u32[]{:S(2)}) collective-permute-start(bf16[128,896]{1,0:T(8,128)(2,1)S(1)} %get-tuple-element.45), channel_id=1, source_target_pairs={{128,0},{144,16},{160,32},{176,48},{192,64},{208,80},{224,96},{240... | collective-permute-start | bytes 688136 | tf_op jit(solution)/shard_map/cond/branch_1_fun/ppermute | solution.py:69
  118.4 4.7 %collective-permute-start.2 = (bf16[128,896]{1,0:T(8,128)(2,1)S(1)}, bf16[128,896]{1,0:T(8,128)(2,1)S(1)}, u32[]{:S(2)}, u32[]{:S(2)}) collective-permute-start(bf16[128,896]{1,0:T(8,128)(2,1)S(1)} %get-tuple-element.44), channel_id=1, source_target_pairs={{256,0},{272,16},{288,32},{304,48},{320,64},{336,80},{352,96},{368... | collective-permute-start | bytes 688136 | tf_op jit(solution)/shard_map/cond/branch_1_fun/ppermute | solution.py:69
  123.0 3.6 %collective-permute-start.1 = (bf16[128,896]{1,0:T(8,128)(2,1)S(1)}, bf16[128,896]{1,0:T(8,128)(2,1)S(1)}, u32[]{:S(2)}, u32[]{:S(2)}) collective-permute-start(bf16[128,896]{1,0:T(8,128)(2,1)S(1)} %get-tuple-element.43), channel_id=1, source_target_pairs={{384,0},{400,16},{416,32},{432,48},{448,64},{464,80},{480,96},{496... | collective-permute-start | bytes 688136 | tf_op jit(solution)/shard_map/cond/branch_1_fun/ppermute | solution.py:69
  126.7 0.9 collective-permute-done.3
  127.6 4.4 %collective-permute-done.2 = bf16[128,896]{1,0:T(8,128)(2,1)S(1)} collective-permute-done((bf16[128,896]{1,0:T(8,128)(2,1)S(1)}, bf16[128,896]{1,0:T(8,128)(2,1)S(1)}, u32[]{:S(2)}, u32[]{:S(2)}) %collective-permute-start.2) | collective-permute-done | bytes 229408 | tf_op jit(solution)/shard_map/cond/branch_1_fun/ppermute | solution.py:69
  131.9 2.5 %collective-permute-done.1 = bf16[128,896]{1,0:T(8,128)(2,1)S(1)} collective-permute-done((bf16[128,896]{1,0:T(8,128)(2,1)S(1)}, bf16[128,896]{1,0:T(8,128)(2,1)S(1)}, u32[]{:S(2)}, u32[]{:S(2)}) %collective-permute-start.1) | collective-permute-done | bytes 229408 | tf_op jit(solution)/shard_map/cond/branch_1_fun/ppermute | solution.py:69
  134.4 1.1 fusion.6
  135.5 2.7 %all-to-all-done.1 = bf16[8,128,128]{2,1,0:T(8,128)(2,1)S(1)} async-done(((bf16[8,128,128]{2,1,0:T(8,128)(2,1)}), bf16[8,128,128]{2,1,0:T(8,128)(2,1)S(1)}, u32[]{:S(2)}, u32[]{:S(2)}) %all-to-all-start.1) | async-done | bytes 262176 | tf_op jit(solution)/shard_map/cond/branch_1_fun/all_to_all | solution.py:82
  138.3 4.6 %collective-permute-start.6 = (bf16[128,256]{1,0:T(8,128)(2,1)S(1)}, bf16[128,256]{1,0:T(8,128)(2,1)S(1)}, u32[]{:S(2)}, u32[]{:S(2)}) collective-permute-start(bf16[128,256]{1,0:T(8,128)(2,1)S(1)} %get-tuple-element.68), channel_id=1, source_target_pairs={{0,0},{1,1},{2,2},{3,3},{128,4},{129,5},{130,6},{131,7},{256,8},{2... | collective-permute-start | bytes 196616 | tf_op jit(solution)/shard_map/ppermute | solution.py:73
  143.0 0.7 multiply_convert_fusion
  143.7 5.5 %collective-permute-done.6 = bf16[128,256]{1,0:T(8,128)(2,1)S(1)} collective-permute-done((bf16[128,256]{1,0:T(8,128)(2,1)S(1)}, bf16[128,256]{1,0:T(8,128)(2,1)S(1)}, u32[]{:S(2)}, u32[]{:S(2)}) %collective-permute-start.6) | collective-permute-done | bytes 65568 | tf_op jit(solution)/shard_map/ppermute | solution.py:73
  149.2 0.0 reduce-scatter.2.cloned.1.call-done
  149.2 1.7 %convert_multiply_fusion = f32[128,896]{1,0:T(8,128)} fusion(bf16[128,896]{1,0:T(8,128)(2,1)} %reduce-scatter.2.cloned.1.call-done), kind=kLoop, calls=%fused_computation.24 | loop fusion | flops 229376 | bytes 688128 | tf_op jit(solution)/shard_map/mul | solution.py:152
  150.9 0.6 copy.18
  (11 shorter events, 0.3 us)
Async XLA Ops:
  7.2 11.1 %collective-permute-start.4 = (bf16[128,256]{1,0:T(8,128)(2,1)}, bf16[128,256]{1,0:T(8,128)(2,1)S(1)}, u32[]{:S(2)}, u32[]{:S(2)}) collective-permute-start(bf16[128,256]{1,0:T(8,128)(2,1)} %param.6), channel_id=1, source_target_pairs={{0,0},{1,1},{2,2},{3,3},{128,4},{129,5},{130,6},{131,7},{256,8},{2... | collective-permute-start | bytes 196616 | tf_op jit(solution)/shard_map/ppermute | solution.py:73
  19.0 15.6 %all-to-all-start.2 = ((bf16[8,128,128]{2,1,0:T(8,128)(2,1)}), bf16[8,128,128]{2,1,0:T(8,128)(2,1)S(1)}, u32[]{:S(2)}, u32[]{:S(2)}) async-start(bf16[8,128,128]{2,1,0:T(8,128)(2,1)} %bitcast.21), calls=%async_computation.2 | async-start | bytes 524288 | tf_op jit(solution)/shard_map/all_to_all | solution.py:82
  24.9 56.8 %all-gather.2.cloned.1.call-start = ((), (), s32[]{:S(2)}) async-start(), calls=%async_computation.5 | async-start | bytes 2293760 | tf_op jit(solution)/shard_map/all_gather | solution.py:140
  26.7 3.5 %collective-permute-start.5 = (bf16[128,896]{1,0:T(8,128)(2,1)S(1)}, bf16[128,896]{1,0:T(8,128)(2,1)S(1)}, u32[]{:S(2)}, u32[]{:S(2)}) collective-permute-start(bf16[128,896]{1,0:T(8,128)(2,1)S(1)} %multiply_convert_fusion.1), channel_id=1, source_target_pairs={{16,0},{0,16},{48,32},{32,48},{80,64},{64,80},{112,96},{96,112},{1... | collective-permute-start | bytes 688136 | tf_op jit(solution)/shard_map/ppermute | solution.py:65
  34.8 4.7 %copy-start = (bf16[128,896]{1,0:T(8,128)(2,1)S(1)}, bf16[128,896]{1,0:T(8,128)(2,1)}, u32[]{:S(2)}) copy-start(bf16[128,896]{1,0:T(8,128)(2,1)} %param.7) | copy-start | bytes 688132
  35.9 45.8 %all-to-all-start.3 = ((bf16[4,2,128,512]{3,2,1,0:T(8,128)(2,1)}), bf16[4,2,128,512]{3,2,1,0:T(8,128)(2,1)S(1)}, u32[]{:S(2)}, u32[]{:S(2)}) async-start(bf16[4,2,128,512]{3,2,1,0:T(8,128)(2,1)} %broadcast_in_dim.5), calls=%async_computation.3 | async-start | bytes 2097152 | tf_op jit(solution)/shard_map/all_to_all | solution.py:82
  39.4 109.8 %reduce-scatter.2.cloned.1.call-start = ((), (), s32[]{:S(2)}) async-start(), calls=%async_computation.6 | async-start | bytes 1146880 | tf_op jit(solution)/shard_map/reduce_scatter | solution.py:148
  89.2 19.7 %all-to-all-start = ((bf16[4,2,128,512]{3,2,1,0:T(8,128)(2,1)}), bf16[4,2,128,512]{3,2,1,0:T(8,128)(2,1)}, u32[]{:S(2)}, u32[]{:S(2)}) async-start(bf16[4,2,128,512]{3,2,1,0:T(8,128)(2,1)} %bitcast.10), calls=%async_computation | async-start | bytes 2097152 | tf_op jit(solution)/shard_map/cond/branch_1_fun/all_to_all | solution.py:82
  95.8 15.5 %collective-permute-start = (bf16[4,128,896]{2,1,0:T(8,128)(2,1)S(1)}, bf16[4,128,896]{2,1,0:T(8,128)(2,1)}, u32[]{:S(2)}, u32[]{:S(2)}) collective-permute-start(bf16[4,128,896]{2,1,0:T(8,128)(2,1)S(1)} %fusion), channel_id=1, source_target_pairs={{16,0},{0,16},{48,32},{32,48},{80,64},{64,80},{112,96},{96,112},{1... | collective-permute-start | bytes 2752520 | tf_op jit(solution)/shard_map/cond/branch_1_fun/ppermute | solution.py:65
  112.6 25.6 %all-to-all-start.1 = ((bf16[8,128,128]{2,1,0:T(8,128)(2,1)}), bf16[8,128,128]{2,1,0:T(8,128)(2,1)S(1)}, u32[]{:S(2)}, u32[]{:S(2)}) async-start(bf16[8,128,128]{2,1,0:T(8,128)(2,1)} %bitcast.15), calls=%async_computation.1 | async-start | bytes 524288 | tf_op jit(solution)/shard_map/cond/branch_1_fun/all_to_all | solution.py:82
  116.0 11.6 %collective-permute-start.3 = (bf16[128,896]{1,0:T(8,128)(2,1)S(1)}, bf16[128,896]{1,0:T(8,128)(2,1)S(1)}, u32[]{:S(2)}, u32[]{:S(2)}) collective-permute-start(bf16[128,896]{1,0:T(8,128)(2,1)S(1)} %get-tuple-element.45), channel_id=1, source_target_pairs={{128,0},{144,16},{160,32},{176,48},{192,64},{208,80},{224,96},{240... | collective-permute-start | bytes 688136 | tf_op jit(solution)/shard_map/cond/branch_1_fun/ppermute | solution.py:69
  118.4 13.5 %collective-permute-start.2 = (bf16[128,896]{1,0:T(8,128)(2,1)S(1)}, bf16[128,896]{1,0:T(8,128)(2,1)S(1)}, u32[]{:S(2)}, u32[]{:S(2)}) collective-permute-start(bf16[128,896]{1,0:T(8,128)(2,1)S(1)} %get-tuple-element.44), channel_id=1, source_target_pairs={{256,0},{272,16},{288,32},{304,48},{320,64},{336,80},{352,96},{368... | collective-permute-start | bytes 688136 | tf_op jit(solution)/shard_map/cond/branch_1_fun/ppermute | solution.py:69
  123.0 11.4 %collective-permute-start.1 = (bf16[128,896]{1,0:T(8,128)(2,1)S(1)}, bf16[128,896]{1,0:T(8,128)(2,1)S(1)}, u32[]{:S(2)}, u32[]{:S(2)}) collective-permute-start(bf16[128,896]{1,0:T(8,128)(2,1)S(1)} %get-tuple-element.43), channel_id=1, source_target_pairs={{384,0},{400,16},{416,32},{432,48},{448,64},{464,80},{480,96},{496... | collective-permute-start | bytes 688136 | tf_op jit(solution)/shard_map/cond/branch_1_fun/ppermute | solution.py:69
  138.3 10.9 %collective-permute-start.6 = (bf16[128,256]{1,0:T(8,128)(2,1)S(1)}, bf16[128,256]{1,0:T(8,128)(2,1)S(1)}, u32[]{:S(2)}, u32[]{:S(2)}) collective-permute-start(bf16[128,256]{1,0:T(8,128)(2,1)S(1)} %get-tuple-element.68), channel_id=1, source_target_pairs={{0,0},{1,1},{2,2},{3,3},{128,4},{129,5},{130,6},{131,7},{256,8},{2... | collective-permute-start | bytes 196616 | tf_op jit(solution)/shard_map/ppermute | solution.py:73
Sparse Core Ops, SparseCore 0:
  34.9 33.9 all-gather.1
  85.6 54.1 reduce-scatter.1
